TPU v7x, 32 devices: a whole 2x2x4 slice. The times are simulated.
32 devices in a mesh: dp: 2 (over x), seq: 16 (over z, y, core).
Axes of the slice: x: 2, y: 2, z: 4, core: 2. Of those that a mesh axis runs over, the one named last changes fastest.
Arguments:
- inputs: bfloat16 [2, 16384, 1024], P('dp', 'seq'), may hold values from -6 to 6
- cotangent: bfloat16 [2, 16384, 1024], P('dp', 'seq'), may hold values from -4 to 4
- factor_one: bfloat16 [16, 1024, 1024], P('seq'), may hold values from -0.1875 to 0.1875
- factor_two: bfloat16 [16, 1024, 1024], P('seq'), may hold values from -0.1875 to 0.1875
Outputs:
- mixed: bfloat16 [2, 16384, 1024], P('dp', 'seq')
- grad_input: bfloat16 [2, 16384, 1024], P('dp', 'seq')
- grad_one: float32 [16, 1024, 1024], P('seq', 'dp')
- grad_two: float32 [16, 1024, 1024], P('seq', 'dp')
All inputs are finite; a program needn't handle non-finite values.
Results may differ from a plain program's by a relative error of at most 0.014.
Values may be sent and summed in bfloat16 or wider, within the bound.
A program may use at most 128 MiB of HBM per device.

v0:
```python
import jax
import jax.numpy as jnp
from jax import lax
from jax.sharding import PartitionSpec as P


def local(inputs, cotangent, factor_one, factor_two):
    seqs, block, width = inputs.shape
    count = lax.axis_size("seq")
    rows = block // count
    fone = factor_one[0]
    ftwo = factor_two[0]
    xfull = inputs.astype(jnp.float32)
    dyfull = cotangent.astype(jnp.float32)
    first = jnp.einsum("kj,sjc->skc", fone, inputs, preferred_element_type=jnp.float32).astype(
        jnp.bfloat16
    )
    gated = (dyfull * xfull).astype(jnp.bfloat16)
    moved = lax.all_to_all(
        first.reshape(seqs, count, rows, 1, width), "seq", split_axis=1, concat_axis=3, tiled=True
    )
    moved = moved.reshape(seqs, block, width)
    second = jnp.einsum("pq,sqc->spc", ftwo, moved, preferred_element_type=jnp.float32).astype(
        jnp.bfloat16
    )
    monarch = lax.all_to_all(
        second.reshape(seqs, 1, rows, count, width), "seq", split_axis=3, concat_axis=1, tiled=True
    )
    monarch = monarch.reshape(seqs, block, width)
    gated_moved = lax.all_to_all(
        gated.reshape(seqs, count, rows, 1, width), "seq", split_axis=1, concat_axis=3, tiled=True
    )
    gated_moved = gated_moved.reshape(seqs, block, width)
    back_two = jnp.einsum(
        "pq,spc->sqc", ftwo, gated_moved, preferred_element_type=jnp.float32
    ).astype(jnp.bfloat16)
    back_moved = lax.all_to_all(
        back_two.reshape(seqs, 1, rows, count, width),
        "seq",
        split_axis=3,
        concat_axis=1,
        tiled=True,
    )
    back_moved = back_moved.reshape(seqs, block, width)
    mfull = monarch.astype(jnp.float32)
    mixed = (xfull * mfull).astype(jnp.bfloat16)
    part_two = jnp.einsum("spc,sqc->pq", gated_moved, moved, preferred_element_type=jnp.float32)
    part_one = jnp.einsum("skc,sjc->kj", back_moved, inputs, preferred_element_type=jnp.float32)
    grad_one, grad_two = (
        lax.psum_scatter(
            part_one.astype(jnp.bfloat16), "dp", scatter_dimension=0, tiled=True
        ).astype(jnp.float32),
        lax.psum_scatter(
            part_two.astype(jnp.bfloat16), "dp", scatter_dimension=0, tiled=True
        ).astype(jnp.float32),
    )
    spread = jnp.einsum("kj,skc->sjc", fone, back_moved, preferred_element_type=jnp.float32)
    grad_input = (dyfull * mfull + spread).astype(jnp.bfloat16)
    return (mixed, grad_input, grad_one[None], grad_two[None])


def solution(mesh):
    in_specs = (
        P("dp", "seq", None),
        P("dp", "seq", None),
        P("seq", None, None),
        P("seq", None, None),
    )
    out_specs = (
        P("dp", "seq", None),
        P("dp", "seq", None),
        P("seq", "dp", None),
        P("seq", "dp", None),
    )
    return jax.shard_map(local, mesh=mesh, in_specs=in_specs, out_specs=out_specs, check_vma=False)
```

profile of v0, /device:TPU:16, one launch (start us, length us, event | category | flops | bytes accessed | tf_op | source)
XLA Modules:
  0.0 301.8 jit_solution(4284375883617256523)
XLA Ops:
  7.2 0.0 copy-start
  7.2 4.7 %fusion.17 = bf16[1024,1024]{0,1:T(8,128)(2,1)S(1)} fusion(bf16[1,1024,1024]{2,1,0:T(8,128)(2,1)} %param.4, bf16[1,1024,1024]{2,1,0:T(8,128)(2,1)} %param.6), kind=kOutput, calls=%fused_computation.19 | convolution fusion | flops 2148532224 | bytes 6291456 | tf_op jit(solution)/shard_map/kj,sjc->skc/dot_general | solution.py:15
  11.9 53.6 %all_to_all.54 = bf16[1,16,64,1,1024]{4,2,3,0,1:T(8,128)(2,1)S(1)} all-to-all(bf16[1,16,64,1,1024]{4,2,3,0,1:T(8,128)(2,1)S(1)} %bitcast.90), channel_id=1, replica_groups=mesh['dp'=2,'seq'=16] {'seq'}, dimensions={1} | all-to-all | bytes 4194304 | tf_op jit(solution)/shard_map/all_to_all | solution.py:19
  65.5 1.2 copy.26
  66.6 0.0 copy-start.4
  66.6 0.0 copy-done
  66.6 2.4 fusion.22
  69.0 0.0 copy-done.4
  69.0 2.5 copy.27
  71.5 4.8 %all-to-all-start.1 = ((bf16[1,1,64,16,1024]{4,2,1,0,3:T(8,128)(2,1)}), bf16[1,1,64,16,1024]{4,2,1,0,3:T(8,128)(2,1)}, u32[]{:S(2)}, u32[]{:S(2)}) async-start(bf16[1,1,64,16,1024]{4,2,1,0,3:T(8,128)(2,1)} %copy.27), calls=%async_computation.1 | async-start | bytes 4194304 | tf_op jit(solution)/shard_map/all_to_all | solution.py:26
  76.3 3.9 %copy.24 = bf16[1,1024,1024]{1,2,0:T(8,128)(2,1)} copy(bf16[1,1024,1024]{2,1,0:T(8,128)(2,1)} %param.4) | data formatting | bytes 4194304 | tf_op args[0]
  80.3 3.9 %copy.30 = bf16[1,1024,1024]{1,2,0:T(8,128)(2,1)} copy(bf16[1,1024,1024]{2,1,0:T(8,128)(2,1)} %param.5) | data formatting | bytes 4194304 | tf_op args[1]
  84.2 39.9 %all-to-all-done.1 = bf16[1,1,64,16,1024]{4,2,1,0,3:T(8,128)(2,1)} async-done(((bf16[1,1,64,16,1024]{4,2,1,0,3:T(8,128)(2,1)}), bf16[1,1,64,16,1024]{4,2,1,0,3:T(8,128)(2,1)}, u32[]{:S(2)}, u32[]{:S(2)}) %all-to-all-start.1) | async-done | bytes 2097184 | tf_op jit(solution)/shard_map/all_to_all | solution.py:26
  124.1 4.0 %bitcast_convert_fusion = f32[1,1,64,16,1,1024]{5,2,3,4,1,0:T(8,128)} fusion(bf16[1,1,64,16,1024]{4,2,1,0,3:T(8,128)(2,1)} %all-to-all-done.1), kind=kLoop, calls=%fused_computation.7 | loop fusion | flops 1048576 | bytes 6291456 | tf_op jit(solution)/shard_map/convert_element_type | solution.py:45
  128.1 5.4 %copy.29 = f32[1,1024,1024]{1,2,0:T(8,128)} copy(f32[1,1024,1024]{2,1,0:T(8,128)} %bitcast.84) | data formatting | bytes 8388608 | tf_op jit(solution)/shard_map/convert_element_type | solution.py:45
  133.5 6.9 %fusion.3 = (bf16[1,1024,1024]{1,2,0:T(8,128)(2,1)}, bf16[1,1024,1024]{1,2,0:T(8,128)(2,1)}) fusion(bf16[1,1024,1024]{1,2,0:T(8,128)(2,1)} %copy.24, bf16[1,1024,1024]{1,2,0:T(8,128)(2,1)} %copy.30, f32[1,1024,1024]{1,2,0:T(8,128)} %copy.29), kind=kLoop, calls=%fused_computation.6 | loop fusion | flops 6291456 | bytes 12582912 | tf_op jit(solution)/shard_map/convert_element_type | solution.py:18
  140.3 3.9 %copy.32 = bf16[1,1024,1024]{2,1,0:T(8,128)(2,1)} copy(bf16[1,1024,1024]{1,2,0:T(8,128)(2,1)} %get-tuple-element.16) | data formatting | bytes 4194304 | tf_op jit(solution)/shard_map/convert_element_type | solution.py:18
  144.2 52.3 %all_to_all.55 = bf16[1,16,64,1,1024]{4,2,3,0,1:T(8,128)(2,1)S(1)} all-to-all(bf16[1,16,64,1,1024]{4,2,3,0,1:T(8,128)(2,1)} %bitcast.85), channel_id=1, replica_groups=mesh['dp'=2,'seq'=16] {'seq'}, dimensions={1} | all-to-all | bytes 4194304 | tf_op jit(solution)/shard_map/all_to_all | solution.py:30
  196.5 1.2 copy.34
  197.7 0.0 copy-start.6
  197.7 2.4 fusion.25
  200.1 0.0 copy-done.6
  200.1 2.5 copy.35
  202.6 0.0 copy-start.5
  202.6 5.0 %all-to-all-start.3 = ((bf16[1,1,64,16,1024]{4,2,1,0,3:T(8,128)(2,1)}), bf16[1,1,64,16,1024]{4,2,1,0,3:T(8,128)(2,1)}, u32[]{:S(2)}, u32[]{:S(2)}) async-start(bf16[1,1,64,16,1024]{4,2,1,0,3:T(8,128)(2,1)} %copy.35), calls=%async_computation.3 | async-start | bytes 4194304 | tf_op jit(solution)/shard_map/all_to_all | solution.py:37
  207.6 0.0 reduce-scatter.5.cloned.1.call-start
  207.6 0.0 copy-done.5
  207.6 5.3 %convolution_convert_fusion = bf16[1024,1024]{1,0:T(8,128)(2,1)} fusion(bf16[1024,1024]{1,0:T(8,128)(2,1)} %bitcast.89, bf16[1024,1024]{1,0:T(8,128)(2,1)S(1)} %bitcast.87), kind=kOutput, calls=%fused_computation.22 | convolution fusion | flops 2148532224 | bytes 6291456 | tf_op jit(solution)/shard_map/spc,sqc->pq/dot_general | solution.py:47
  213.0 0.0 copy-start.3
  213.0 0.0 reduce-scatter.5.cloned.1.call-update
  213.0 0.3 reduce-scatter.3.cloned.1.call-start
  213.3 42.1 %all-to-all-done.3 = bf16[1,1,64,16,1024]{4,2,1,0,3:T(8,128)(2,1)} async-done(((bf16[1,1,64,16,1024]{4,2,1,0,3:T(8,128)(2,1)}), bf16[1,1,64,16,1024]{4,2,1,0,3:T(8,128)(2,1)}, u32[]{:S(2)}, u32[]{:S(2)}) %all-to-all-start.3) | async-done | bytes 2097184 | tf_op jit(solution)/shard_map/all_to_all | solution.py:37
  255.3 0.0 copy-done.3
  255.3 5.3 %fusion.14 = bf16[1024,1024]{1,0:T(8,128)(2,1)} fusion(bf16[1024,1024]{1,0:T(8,128)(2,1)} %bitcast.29, bf16[1,1024,1024]{2,1,0:T(8,128)(2,1)S(1)} %copy-done.3), kind=kOutput, calls=%fused_computation.18 | convolution fusion | flops 2148532224 | bytes 6291456 | tf_op jit(solution)/shard_map/skc,sjc->kj/dot_general | solution.py:48
  260.6 0.0 reduce-scatter.3.cloned.1.call-update
  260.7 0.0 copy-start.2
  260.7 4.1 %copy.36 = bf16[1,1024,1024]{2,1,0:T(8,128)(2,1)} copy(bf16[1,1024,1024]{1,2,0:T(8,128)(2,1)} %get-tuple-element.17) | data formatting | bytes 4194304
  264.8 0.0 copy-done.2
  264.8 7.9 %fusion.2 = bf16[1,1024,1024]{1,2,0:T(8,128)(2,1)} fusion(f32[1,1024,1024]{1,2,0:T(8,128)} %copy.29, bf16[1,1024,1024]{1,2,0:T(8,128)(2,1)S(1)} %copy-done.2, bf16[1024,1024]{1,0:T(8,128)(2,1)} %bitcast.29, bf16[1,1024,1024]{2,1,0:T(8,128)(2,1)} %param.6), kind=kOutput, calls=%fused_computation.5 | convolution fusion | flops 2151677952 | bytes 12582912 | tf_op jit(solution)/shard_map/kj,skc->sjc/dot_general | solution.py:57
  272.7 3.9 %copy.37 = bf16[1,1024,1024]{2,1,0:T(8,128)(2,1)} copy(bf16[1,1024,1024]{1,2,0:T(8,128)(2,1)} %fusion.2) | data formatting | bytes 4194304
  276.6 0.0 reduce-scatter.5.cloned.1.call-done
  276.6 0.0 copy-start.1
  276.6 2.9 bitcast_convert_fusion.1
  279.6 12.6 %reduce-scatter.3.cloned.1.call-done = bf16[512,1024]{1,0:T(8,128)(2,1)} async-done(((bf16[1024,1024]{1,0:T(8,128)(2,1)}), bf16[512,1024]{1,0:T(8,128)(2,1)}) %reduce-scatter.3.cloned.1.call-update) | async-done | bytes 1048592 | tf_op jit(solution)/shard_map/reduce_scatter | solution.py:50
  292.2 2.8 bitcast_convert_fusion.2
  295.0 0.0 copy-done.1
Async XLA Ops:
  7.2 59.5 %copy-start = (bf16[1,1024,1024]{2,1,0:T(8,128)(2,1)S(1)}, bf16[1,1024,1024]{2,1,0:T(8,128)(2,1)}, u32[]{:S(2)}) copy-start(bf16[1,1024,1024]{2,1,0:T(8,128)(2,1)} %param.7) | copy-start | bytes 6291460
  66.6 2.4 copy-start.4
  71.5 52.6 %all-to-all-start.1 = ((bf16[1,1,64,16,1024]{4,2,1,0,3:T(8,128)(2,1)}), bf16[1,1,64,16,1024]{4,2,1,0,3:T(8,128)(2,1)}, u32[]{:S(2)}, u32[]{:S(2)}) async-start(bf16[1,1,64,16,1024]{4,2,1,0,3:T(8,128)(2,1)} %copy.27), calls=%async_computation.1 | async-start | bytes 4194304 | tf_op jit(solution)/shard_map/all_to_all | solution.py:26
  197.7 2.4 copy-start.6
  202.6 5.0 %copy-start.5 = (bf16[1,16,64,1,1024]{4,1,2,3,0:T(8,128)(2,1)S(1)}, bf16[1,16,64,1,1024]{4,1,2,3,0:T(8,128)(2,1)}, u32[]{:S(2)}) copy-start(bf16[1,16,64,1,1024]{4,1,2,3,0:T(8,128)(2,1)} %copy-done.4) | copy-start | bytes 6291460
  202.6 52.7 %all-to-all-start.3 = ((bf16[1,1,64,16,1024]{4,2,1,0,3:T(8,128)(2,1)}), bf16[1,1,64,16,1024]{4,2,1,0,3:T(8,128)(2,1)}, u32[]{:S(2)}, u32[]{:S(2)}) async-start(bf16[1,1,64,16,1024]{4,2,1,0,3:T(8,128)(2,1)} %copy.35), calls=%async_computation.3 | async-start | bytes 4194304 | tf_op jit(solution)/shard_map/all_to_all | solution.py:37
  207.6 69.1 %reduce-scatter.5.cloned.1.call-start = ((), (), s32[]{:S(2)}) async-start(), calls=%async_computation.7 | async-start | bytes 3145728 | tf_op jit(solution)/shard_map/reduce_scatter | solution.py:53
  213.0 42.4 %copy-start.3 = (bf16[1,1024,1024]{2,1,0:T(8,128)(2,1)S(1)}, bf16[1,1024,1024]{2,1,0:T(8,128)(2,1)}, u32[]{:S(2)}) copy-start(bf16[1,1024,1024]{2,1,0:T(8,128)(2,1)} %param.4) | copy-start | bytes 6291460
  213.0 79.2 %reduce-scatter.3.cloned.1.call-start = ((), (), s32[]{:S(2)}) async-start(), calls=%async_computation.6 | async-start | bytes 3145728 | tf_op jit(solution)/shard_map/reduce_scatter | solution.py:50
  260.7 4.1 %copy-start.2 = (bf16[1,1024,1024]{1,2,0:T(8,128)(2,1)S(1)}, bf16[1,1024,1024]{1,2,0:T(8,128)(2,1)}, u32[]{:S(2)}) copy-start(bf16[1,1024,1024]{1,2,0:T(8,128)(2,1)} %copy.30) | copy-start | bytes 6291460
  276.6 18.3 %copy-start.1 = (bf16[1,1024,1024]{2,1,0:T(8,128)(2,1)S(1)}, bf16[1,1024,1024]{2,1,0:T(8,128)(2,1)}, u32[]{:S(2)}) copy-start(bf16[1,1024,1024]{2,1,0:T(8,128)(2,1)} %param.7) | copy-start | bytes 6291460
Sparse Core Ops, SparseCore 0:
  213.1 32.7 reduce-scatter.4
  260.8 31.3 reduce-scatter.2
where the time goes:
time: 304 us; the launch traced here: 302 us
  blocking collectives  106 us (35%)
  waiting for transfers between devices  94.6 us (31%)
  local copies, waits for them, and re-layouts  32.5 us (11%)
  matrix products  28.1 us (9%)
  other arithmetic  16.6 us (5%)
  between operations  14.1 us (5%)
  starting transfers between devices  10.1 us (3%)
    all_to_all x1, blocking collectives, local(): lax.all_to_all(first.reshape(seqs, count, rows, 1, width), 'seq', split_a...  53.6 us
    all_to_all x1, blocking collectives, local(): lax.all_to_all(gated.reshape(seqs, count, rows, 1, width), 'seq', split_a...  52.3 us
    all_to_all x1, waiting for transfers between devices, local(): lax.all_to_all(back_two.reshape(seqs, 1, rows, count, width), 'seq', spli...  42.1 us
    all_to_all x1, waiting for transfers between devices, local(): lax.all_to_all(second.reshape(seqs, 1, rows, count, width), 'seq', split_...  39.9 us
    unnamed x18, local copies, waits for them, and re-layouts  15.9 us
    reduce_scatter x1, waiting for transfers between devices, local(): lax.psum_scatter(part_one.astype(jnp.bfloat16), 'dp', scatter_dimension=0...  12.6 us
    dot_general x1, matrix products, local(): jnp.einsum('kj,skc->sjc', fone, back_moved, preferred_element_type=jnp.fl...  7.94 us
    convert_element_type x1, other arithmetic, local(): gated = (dyfull * xfull).astype(jnp.bfloat16)  6.85 us
  transfers between devices with their start and end apart: 4, of which 3 were waited for; matrix products, arithmetic and copies ran while one was open for 12% of the time, Pallas kernels for 0%

commit v1 on v0

v1 whole, which is shorter than its diff:
```python
import functools

import jax
import jax.numpy as jnp
from jax import lax
from jax.experimental import pallas as pl
from jax.experimental.pallas import tpu as pltpu
from jax.sharding import PartitionSpec as P

MESH = pl.DeviceIdType.MESH
F32 = jnp.float32
BF16 = jnp.bfloat16

CHUNKS = 4
TILE = 256
DEPTH = 3

GATED, FIRST, BACK, SECOND = range(4)


def nn(a, b):
    return jnp.dot(a, b, preferred_element_type=F32)


def nt(a, b):
    return lax.dot_general(a, b, (((1,), (1,)), ((), ())), preferred_element_type=F32)


def loop(n, body):
    def step(i, carry):
        body(i)
        return carry

    lax.fori_loop(0, n, step, 0)


def kernel(
    count,
    ndp,
    x_hbm,
    c_hbm,
    f1_hbm,
    f2_hbm,
    mixed_hbm,
    gin_hbm,
    g1_hbm,
    g2_hbm,
    xv,
    cv,
    f1,
    f1t,
    f2,
    f2p,
    f2pt,
    tmp,
    send0,
    send1,
    send2,
    send3,
    recv0,
    recv1,
    recv2,
    recv3,
    spread,
    p1,
    p2,
    r1,
    r2,
    g1,
    g2,
    ssem,
    rsem,
    dssem,
    drsem,
    insem,
    outsem,
):
    sends = (send0, send1, send2, send3)
    recvs = (recv0, recv1, recv2, recv3)
    parts = (p1, p2)
    others = (r1, r2)
    chunks, block, width = xv.shape
    tiles = block // TILE
    rows = block // count
    piece = block // ndp
    dp = lax.axis_index("dp")
    me = lax.axis_index("seq")

    def rowsof(t):
        return pl.ds(pl.multiple_of(t * TILE, TILE), TILE)

    def load(src, dst, i):
        return pltpu.make_async_copy(src, dst, insem.at[i])

    loads = []
    for n in range(chunks):
        cols = pl.ds(n * width, width)
        loads.append(load(x_hbm.at[:, cols], xv.at[n], 2 * n))
        loads.append(load(c_hbm.at[:, cols], cv.at[n], 2 * n + 1))
    load_f1 = load(f1_hbm, f1, 2 * chunks)
    load_f2 = load(f2_hbm, f2, 2 * chunks + 1)
    for copy in loads:
        copy.start()
    load_f1.start()
    load_f2.start()

    barrier = pltpu.get_barrier_semaphore()

    def greet_seq(i):
        pl.semaphore_signal(
            barrier, inc=1, device_id=(dp, (me + 1 + i) % count), device_id_type=MESH
        )

    def greet_dp(i):
        pl.semaphore_signal(
            barrier, inc=1, device_id=((dp + 1 + i) % ndp, me), device_id_type=MESH
        )

    loop(count - 1, greet_seq)
    loop(ndp - 1, greet_dp)

    def seq_copy(t, n, source, target, size, to):
        return pltpu.make_async_remote_copy(
            src_ref=sends[t].at[n, pl.ds(source, size)],
            dst_ref=recvs[t].at[n, pl.ds(target, size)],
            send_sem=ssem.at[t, n],
            recv_sem=rsem.at[t, n],
            device_id=(dp, to),
            device_id_type=MESH,
        )

    mine = pl.multiple_of(me * rows, rows)

    def send(t, n):
        def one(i):
            offset = count // 2 + ((i + 1) // 2) * (1 - 2 * (i % 2))
            to = (me + offset) % count
            seq_copy(t, n, pl.multiple_of(to * rows, rows), mine, rows, to).start()

        loop(count - 1, one)
        recvs[t][n, pl.ds(mine, rows), :] = sends[t][n, pl.ds(mine, rows), :]

    def whole(t, n):
        return seq_copy(t, n, 0, 0, (count - 1) * rows, (me + 1) % count)

    def dp_copy(g, source, target, size, to):
        return pltpu.make_async_remote_copy(
            src_ref=parts[g].at[pl.ds(source, size)],
            dst_ref=others[g].at[pl.ds(target, size)],
            send_sem=dssem.at[g],
            recv_sem=drsem.at[g],
            device_id=(to, me),
            device_id_type=MESH,
        )

    own = pl.multiple_of(dp * piece, piece)

    def dp_send(g):
        def one(i):
            to = (dp + 1 + i) % ndp
            dp_copy(g, pl.multiple_of(to * piece, piece), own, piece, to).start()

        loop(ndp - 1, one)

    def dp_whole(g):
        return dp_copy(g, 0, 0, (ndp - 1) * piece, (dp + 1) % ndp)

    def dp_finish(g, out, out_hbm):
        dp_whole(g).wait_recv()
        others[g][pl.ds(own, piece), :] = parts[g][pl.ds(own, piece), :]
        step = min(piece, 128)

        def add(i):
            total = others[g][pl.ds(pl.multiple_of(i * step, step), step), :].astype(F32)
            for d in range(1, ndp):
                at = pl.multiple_of(d * piece + i * step, step)
                total += others[g][pl.ds(at, step), :].astype(F32)
            out[pl.ds(pl.multiple_of(i * step, step), step), :] = total

        loop(piece // step, add)
        copy = pltpu.make_async_copy(out, out_hbm, outsem.at[2 * chunks + g])
        copy.start()
        return copy

    shift = count.bit_length() - 1
    back_shift = rows.bit_length() - 1

    def select(t, forth):
        row = lax.broadcasted_iota(jnp.int32, (TILE, block), 0) + t * TILE
        col = lax.broadcasted_iota(jnp.int32, (TILE, block), 1)
        if forth:
            want = (row & (rows - 1)) * count + lax.shift_right_logical(
                row, jnp.full_like(row, back_shift)
            )
        else:
            want = (row & (count - 1)) * rows + lax.shift_right_logical(
                row, jnp.full_like(row, shift)
            )
        return jnp.where(col == want, 1.0, 0.0).astype(BF16)

    def identity(t):
        row = lax.broadcasted_iota(jnp.int32, (TILE, block), 0) + t * TILE
        col = lax.broadcasted_iota(jnp.int32, (TILE, block), 1)
        return jnp.where(col == row, 1.0, 0.0).astype(BF16)

    def make_gated(n):
        def tile(t):
            s = rowsof(t)
            send0[n, s, :] = (cv[n, s, :].astype(F32) * xv[n, s, :].astype(F32)).astype(BF16)

        loop(tiles, tile)

    def make_product(left, right, out, n):
        def tile(t):
            s = rowsof(t)
            out[n, s, :] = nn(left[s, :], right[n]).astype(out.dtype)

        loop(tiles, tile)

    def arrange_factors():
        def flip(t):
            f1t[rowsof(t), :] = nt(identity(t), f1[...]).astype(BF16)

        loop(tiles, flip)

        load_f2.wait()

        def one(t):
            tmp[rowsof(t), :] = nn(select(t, True), f2[...]).astype(BF16)

        def two(t):
            f2pt[rowsof(t), :] = nt(select(t, True), tmp[...]).astype(BF16)

        def three(t):
            tmp[rowsof(t), :] = nt(select(t, True), f2[...]).astype(BF16)

        def four(t):
            f2p[rowsof(t), :] = nt(select(t, True), tmp[...]).astype(BF16)

        loop(tiles, one)
        loop(tiles, two)
        loop(tiles, three)
        loop(tiles, four)

    def grad_two_part():
        def outer(t):
            s = rowsof(t)
            total = nt(recv0[0, s, :], recv1[0])
            for n in range(1, chunks):
                total += nt(recv0[n, s, :], recv1[n])
            p2[s, :] = total.astype(BF16)

        def one(t):
            tmp[rowsof(t), :] = nt(select(t, False), p2[...]).astype(BF16)

        def two(t):
            p2[rowsof(t), :] = nt(select(t, False), tmp[...]).astype(BF16)

        loop(tiles, outer)
        loop(tiles, one)
        loop(tiles, two)

    def grad_one_part():
        def outer(t):
            s = rowsof(t)
            total = nt(recv2[0, s, :], xv[0])
            for n in range(1, chunks):
                total += nt(recv2[n, s, :], xv[n])
            p1[s, :] = total.astype(BF16)

        loop(tiles, outer)

    half = chunks // 2
    units = [(GATED, n) for n in range(chunks)]
    units += [(FIRST, n) for n in range(half)]
    units += [(BACK, n) for n in range(chunks)]
    units += [(FIRST, n) for n in range(half, chunks)]
    units += [(SECOND, n) for n in range(chunks)]

    def prepare(t, n):
        if t == GATED:
            loads[2 * n].wait()
            loads[2 * n + 1].wait()
            make_gated(n)
        elif t == FIRST:
            if n == 0:
                load_f1.wait()
            make_product(f1, xv, send1, n)
        elif t == BACK:
            if n == 0:
                arrange_factors()
            whole(GATED, n).wait_recv()
            make_product(f2pt, recv0, send2, n)
        else:
            whole(FIRST, n).wait_recv()
            make_product(f2p, recv1, send3, n)

    for u, (t, n) in enumerate(units):
        prepare(t, n)
        if u == 0:
            pl.semaphore_wait(barrier, count - 1 + ndp - 1)
        if u >= DEPTH:
            whole(*units[u - DEPTH]).wait_send()
        send(t, n)

    for n in range(chunks):
        whole(BACK, n).wait_recv()
    grad_one_part()
    dp_send(0)
    grad_two_part()
    dp_send(1)
    for n in range(chunks):
        make_product(f1t, recv2, spread, n)
    outs = [dp_finish(0, g1, g1_hbm), dp_finish(1, g2, g2_hbm)]

    for n in range(chunks):
        whole(SECOND, n).wait_recv()

        def tile(t, n=n):
            s = rowsof(t)
            monarch = recv3[n, s, :].astype(F32)
            send0[n, s, :] = (xv[n, s, :].astype(F32) * monarch).astype(BF16)
            send1[n, s, :] = (cv[n, s, :].astype(F32) * monarch + spread[n, s, :]).astype(BF16)

        loop(tiles, tile)
        cols = pl.ds(n * width, width)
        for i, (src, dst) in enumerate(((send0, mixed_hbm), (send1, gin_hbm))):
            copy = pltpu.make_async_copy(src.at[n], dst.at[:, cols], outsem.at[2 * n + i])
            copy.start()
            outs.append(copy)

    for t, n in units[len(units) - DEPTH :]:
        whole(t, n).wait_send()
    dp_whole(0).wait_send()
    dp_whole(1).wait_send()
    for copy in outs:
        copy.wait()


def local(inputs, cotangent, factor_one, factor_two):
    _, block, width = inputs.shape
    count = lax.axis_size("seq")
    ndp = lax.axis_size("dp")
    piece = block // ndp
    cut = width // CHUNKS
    chunked = pltpu.VMEM((CHUNKS, block, cut), BF16)
    square = pltpu.VMEM((block, block), BF16)
    spec = pl.BlockSpec(memory_space=pl.ANY)
    mixed, grad_input, grad_one, grad_two = pl.pallas_call(
        functools.partial(kernel, count, ndp),
        out_shape=(
            jax.ShapeDtypeStruct((block, width), BF16),
            jax.ShapeDtypeStruct((block, width), BF16),
            jax.ShapeDtypeStruct((piece, block), F32),
            jax.ShapeDtypeStruct((piece, block), F32),
        ),
        in_specs=[spec] * 4,
        out_specs=[spec] * 4,
        scratch_shapes=[chunked] * 2
        + [square] * 6
        + [chunked] * 8
        + [pltpu.VMEM((CHUNKS, block, cut), F32)]
        + [square] * 4
        + [pltpu.VMEM((piece, block), F32)] * 2
        + [
            pltpu.SemaphoreType.DMA((4, CHUNKS)),
            pltpu.SemaphoreType.DMA((4, CHUNKS)),
            pltpu.SemaphoreType.DMA((2,)),
            pltpu.SemaphoreType.DMA((2,)),
            pltpu.SemaphoreType.DMA((2 * CHUNKS + 2,)),
            pltpu.SemaphoreType.DMA((2 * CHUNKS + 2,)),
        ],
        compiler_params=pltpu.CompilerParams(
            collective_id=0, has_side_effects=True, vmem_limit_bytes=60 * 1024 * 1024
        ),
        cost_estimate=pl.CostEstimate(
            flops=12 * block * block * width, bytes_accessed=24 * block * width, transcendentals=0
        ),
    )(inputs[0], cotangent[0], factor_one[0], factor_two[0])
    return mixed[None], grad_input[None], grad_one[None], grad_two[None]


def solution(mesh):
    in_specs = (
        P("dp", "seq", None),
        P("dp", "seq", None),
        P("seq", None, None),
        P("seq", None, None),
    )
    out_specs = (
        P("dp", "seq", None),
        P("dp", "seq", None),
        P("seq", "dp", None),
        P("seq", "dp", None),
    )
    return jax.shard_map(local, mesh=mesh, in_specs=in_specs, out_specs=out_specs, check_vma=False)
```

time: 304 us -> 231 us (0.76)
  Pallas kernels: 0 us -> 220 us
  blocking collectives: 106 us -> 0 us
  waiting for transfers between devices: 94.6 us -> 0 us
  matrix products: 28.1 us -> 0 us
  local copies, waits for them, and re-layouts: 32.5 us -> 9.25 us
  other arithmetic: 16.6 us -> 0 us
  between operations: 14.1 us -> 0.65 us
  starting transfers between devices: 10.1 us -> 0 us
    pallas_call x0 -> x1, Pallas kernels: none -> 220 us  [local(): pl.pallas_call(functools.partial(kernel, count, ndp), out_shape=(jax.Shap...]
    all_to_all x2 -> x0, blocking collectives: 106 us -> none  [the longest x1 53.6 us: local(): lax.all_to_all(first.reshape(seqs, count, rows, 1, width), 'seq', split_a...]
    all_to_all x2 -> x0, waiting for transfers between devices: 81.9 us -> none  [the longest x1 42.1 us: local(): lax.all_to_all(back_two.reshape(seqs, 1, rows, count, width), 'seq', spli...]
    dot_general x6 -> x0, matrix products: 28.1 us -> none  [the longest x1 7.94 us: local(): jnp.einsum('kj,skc->sjc', fone, back_moved, preferred_element_type=jnp.fl...]
    reduce_scatter x2 -> x0, waiting for transfers between devices: 12.6 us -> none  [the longest x1 12.6 us: local(): lax.psum_scatter(part_one.astype(jnp.bfloat16), 'dp', scatter_dimension=0...]
    convert_element_type x2 -> x0, other arithmetic: 10.9 us -> none  [the longest x1 6.85 us: local(): gated = (dyfull * xfull).astype(jnp.bfloat16)]
    all_to_all x2 -> x0, starting transfers between devices: 9.79 us -> none  [the longest x1 4.97 us: local(): lax.all_to_all(back_two.reshape(seqs, 1, rows, count, width), 'seq', spli...]
    convert_element_type x2 -> x0, local copies, waits for them, and re-layouts: 9.3 us -> none  [the longest x1 5.37 us: local(): mfull = monarch.astype(jnp.float32)]
  transfers between devices with their start and end apart: 4 -> 0, of which waited for: 3 -> 0; matrix products, arithmetic and copies ran while one was open for 12% -> 0% of each run, Pallas kernels for 0% -> 0%
where the time goes in v1:
time: 231 us; the launch traced here: 230 us
  Pallas kernels  220 us (95%)
  local copies, waits for them, and re-layouts  9.25 us (4%)
    pallas_call x1, Pallas kernels, local(): pl.pallas_call(functools.partial(kernel, count, ndp), out_shape=(jax.Shap...  220 us
    unnamed x10, local copies, waits for them, and re-layouts  9.25 us

profile of v1, /device:TPU:16, one launch (start us, length us, event | category | flops | bytes accessed | tf_op | source)
XLA Modules:
  0.0 230.2 jit_solution(14235335178163571915)
XLA Ops:
  0.6 220.3 %shard_map.75 = (bf16[1024,1024]{1,0:T(8,128)(2,1)}, bf16[1024,1024]{1,0:T(8,128)(2,1)}, f32[512,1024]{1,0:T(8,128)}, f32[512,1024]{1,0:T(8,128)}) custom-call(bf16[1024,1024]{1,0:T(8,128)(2,1)} %bitcast.12, bf16[1024,1024]{1,0:T(8,128)(2,1)} %bitcast.13, bf16[1024,1024]{1,0:T(8,128)(2,1)} %bitcast.14, bf16[1024,1024]{1,0:T(8,128)(2,1)} %bitcast.15), custom_call_target="tpu_custom_call" | custom-call | flops 12884901888 | bytes 25165824 | tf_op jit(solution)/shard_map/pallas_call | solution.py:349
  220.9 0.0 copy-start.2
  220.9 3.2 %copy.12 = bf16[1,1024,1024]{2,1,0:T(8,128)(2,1)} copy(bf16[1,1024,1024]{2,1,0:T(8,128)(2,1)} %bitcast.11) | data formatting | bytes 4194304
  224.1 0.0 copy-done.2
  224.1 0.0 copy-start.1
  224.1 1.3 copy.13
  225.5 1.0 copy-done.1
  226.5 0.0 copy-start
  226.5 1.3 copy.14
  227.8 1.0 copy-done
  228.8 1.3 copy.15
Async XLA Ops:
  220.9 3.2 %copy-start.2 = (bf16[1024,1024]{1,0:T(8,128)(2,1)S(1)}, bf16[1024,1024]{1,0:T(8,128)(2,1)}, u32[]{:S(2)}) copy-start(bf16[1024,1024]{1,0:T(8,128)(2,1)} %get-tuple-element.9) | copy-start | bytes 6291460
  224.1 2.3 %copy-start.1 = (f32[512,1024]{1,0:T(8,128)S(1)}, f32[512,1024]{1,0:T(8,128)}, u32[]{:S(2)}) copy-start(f32[512,1024]{1,0:T(8,128)} %get-tuple-element.10) | copy-start | bytes 6291460
  226.5 2.3 %copy-start = (f32[512,1024]{1,0:T(8,128)S(1)}, f32[512,1024]{1,0:T(8,128)}, u32[]{:S(2)}) copy-start(f32[512,1024]{1,0:T(8,128)} %get-tuple-element.11) | copy-start | bytes 6291460

commit v2 on v1

--- a/solution.py
+++ b/solution.py
@@ -99,10 +99,8 @@
         loads.append(load(c_hbm.at[:, cols], cv.at[n], 2 * n + 1))
     load_f1 = load(f1_hbm, f1, 2 * chunks)
     load_f2 = load(f2_hbm, f2, 2 * chunks + 1)
-    for copy in loads:
+    for copy in loads[:2]:
         copy.start()
-    load_f1.start()
-    load_f2.start()
 
     barrier = pltpu.get_barrier_semaphore()
 
@@ -118,6 +116,10 @@
 
     loop(count - 1, greet_seq)
     loop(ndp - 1, greet_dp)
+    for copy in loads[2:]:
+        copy.start()
+    load_f1.start()
+    load_f2.start()
 
     def seq_copy(t, n, source, target, size, to):
         return pltpu.make_async_remote_copy(
@@ -133,8 +135,10 @@
 
     def send(t, n):
         def one(i):
-            offset = count // 2 + ((i + 1) // 2) * (1 - 2 * (i % 2))
-            to = (me + offset) % count
+            j = i // 2
+            far = count // 2 + ((j + 1) // 2) * (2 * (j % 2) - 1)
+            near = (1 - j % 2) * (1 + j // 2) + (j % 2) * (count - 1 - j // 2)
+            to = (me + (1 - i % 2) * far + (i % 2) * near) % count
             seq_copy(t, n, pl.multiple_of(to * rows, rows), mine, rows, to).start()
 
         loop(count - 1, one)
@@ -270,12 +274,13 @@
 
         loop(tiles, outer)
 
-    half = chunks // 2
-    units = [(GATED, n) for n in range(chunks)]
-    units += [(FIRST, n) for n in range(half)]
-    units += [(BACK, n) for n in range(chunks)]
-    units += [(FIRST, n) for n in range(half, chunks)]
-    units += [(SECOND, n) for n in range(chunks)]
+    units = [(t, n) for t in (GATED, FIRST, BACK, SECOND) for n in range(chunks)]
+    seen = set()
+
+    def arrived(t, n):
+        if (t, n) not in seen:
+            seen.add((t, n))
+            whole(t, n).wait_recv()
 
     def prepare(t, n):
         if t == GATED:
@@ -283,16 +288,12 @@
             loads[2 * n + 1].wait()
             make_gated(n)
         elif t == FIRST:
-            if n == 0:
-                load_f1.wait()
             make_product(f1, xv, send1, n)
         elif t == BACK:
-            if n == 0:
-                arrange_factors()
-            whole(GATED, n).wait_recv()
+            arrived(GATED, n)
             make_product(f2pt, recv0, send2, n)
         else:
-            whole(FIRST, n).wait_recv()
+            arrived(FIRST, n)
             make_product(f2p, recv1, send3, n)
 
     for u, (t, n) in enumerate(units):
@@ -302,19 +303,29 @@
         if u >= DEPTH:
             whole(*units[u - DEPTH]).wait_send()
         send(t, n)
-
-    for n in range(chunks):
-        whole(BACK, n).wait_recv()
-    grad_one_part()
-    dp_send(0)
-    grad_two_part()
-    dp_send(1)
+        if u == DEPTH - 1:
+            load_f1.wait()
+            arrange_factors()
+        if u == 2 * chunks + DEPTH - 1:
+            for i in range(chunks):
+                arrived(GATED, i)
+                arrived(FIRST, i)
+            grad_two_part()
+            dp_send(1)
+        if u == 3 * chunks + DEPTH - 1:
+            for i in range(chunks):
+                arrived(BACK, i)
+            grad_one_part()
+            dp_send(0)
+
     for n in range(chunks):
         make_product(f1t, recv2, spread, n)
-    outs = [dp_finish(0, g1, g1_hbm), dp_finish(1, g2, g2_hbm)]
+    outs = [dp_finish(1, g2, g2_hbm)]
 
     for n in range(chunks):
-        whole(SECOND, n).wait_recv()
+        if n == chunks - 1:
+            outs.append(dp_finish(0, g1, g1_hbm))
+        arrived(SECOND, n)
 
         def tile(t, n=n):
             s = rowsof(t)
@@ -335,6 +346,25 @@
     dp_whole(1).wait_send()
     for copy in outs:
         copy.wait()
+
+
+def copy_out(*refs):
+    half = len(refs) // 2
+    for src, dst in zip(refs[:half], refs[half:]):
+        dst[...] = src[...]
+
+
+def hand_over(arrays):
+    steps = 4
+    specs = [pl.BlockSpec((a.shape[0] // steps, a.shape[1]), lambda i: (i, 0)) for a in arrays]
+    return pl.pallas_call(
+        copy_out,
+        grid=(steps,),
+        in_specs=specs,
+        out_specs=specs,
+        out_shape=[jax.ShapeDtypeStruct(a.shape, a.dtype) for a in arrays],
+        compiler_params=pltpu.CompilerParams(vmem_limit_bytes=60 * 1024 * 1024),
+    )(*arrays)
 
 
 def local(inputs, cotangent, factor_one, factor_two):
@@ -346,7 +376,7 @@
     chunked = pltpu.VMEM((CHUNKS, block, cut), BF16)
     square = pltpu.VMEM((block, block), BF16)
     spec = pl.BlockSpec(memory_space=pl.ANY)
-    mixed, grad_input, grad_one, grad_two = pl.pallas_call(
+    results = pl.pallas_call(
         functools.partial(kernel, count, ndp),
         out_shape=(
             jax.ShapeDtypeStruct((block, width), BF16),
@@ -377,7 +407,7 @@
             flops=12 * block * block * width, bytes_accessed=24 * block * width, transcendentals=0
         ),
     )(inputs[0], cotangent[0], factor_one[0], factor_two[0])
-    return mixed[None], grad_input[None], grad_one[None], grad_two[None]
+    return tuple(a[None] for a in hand_over(results))
 
 
 def solution(mesh):

time: 231 us -> 197 us (0.85)
  Pallas kernels: 220 us -> 196 us
  local copies, waits for them, and re-layouts: 9.25 us -> 0 us
    pallas_call x1, Pallas kernels: 220 us -> 189 us  [local(): pl.pallas_call(functools.partial(kernel, count, ndp), out_shape=(jax.Shap...]
    unnamed x10 -> x0, local copies, waits for them, and re-layouts: 9.25 us -> none
    pallas_call x0 -> x1, Pallas kernels: none -> 6.97 us  [hand_over(): pl.pallas_call(copy_out, grid=(steps,), in_specs=specs, out_specs=specs,...]
where the time goes in v2:
time: 197 us; the launch traced here: 196 us
  Pallas kernels  196 us (99%)
    pallas_call x1, Pallas kernels, local(): pl.pallas_call(functools.partial(kernel, count, ndp), out_shape=(jax.Shap...  189 us
    pallas_call x1, Pallas kernels, hand_over(): pl.pallas_call(copy_out, grid=(steps,), in_specs=specs, out_specs=specs,...  6.97 us

profile of v2, /device:TPU:16, one launch (start us, length us, event | category | flops | bytes accessed | tf_op | source)
XLA Modules:
  0.0 196.5 jit_solution(15528620035873541370)
XLA Ops:
  0.6 188.9 %shard_map.75 = (bf16[1024,1024]{1,0:T(8,128)(2,1)}, bf16[1024,1024]{1,0:T(8,128)(2,1)}, f32[512,1024]{1,0:T(8,128)}, f32[512,1024]{1,0:T(8,128)}) custom-call(bf16[1024,1024]{1,0:T(8,128)(2,1)} %bitcast.8, bf16[1024,1024]{1,0:T(8,128)(2,1)} %bitcast.9, bf16[1024,1024]{1,0:T(8,128)(2,1)} %bitcast.10, bf16[1024,1024]{1,0:T(8,128)(2,1)} %bitcast.11), custom_call_target="tpu_custom_call" | custom-call | flops 12884901888 | bytes 25165824 | tf_op jit(solution)/shard_map/pallas_call | solution.py:379
  189.5 7.0 %shard_map.76 = (bf16[1024,1024]{1,0:T(8,128)(2,1)}, bf16[1024,1024]{1,0:T(8,128)(2,1)}, f32[512,1024]{1,0:T(8,128)}, f32[512,1024]{1,0:T(8,128)}) custom-call(bf16[1024,1024]{1,0:T(8,128)(2,1)} %get-tuple-element.12.refs_0_, bf16[1024,1024]{1,0:T(8,128)(2,1)} %get-tuple-element.13.refs_1_, f32[512,1024]{1,0:T(8,128)} %get-tuple-element.14.refs_2_, ...), custom_call_target="tpu_custom_call" | custom-call | tf_op jit(solution)/shard_map/pallas_call | solution.py:360

commit v3 on v2

--- a/solution.py
+++ b/solution.py
@@ -41,10 +41,10 @@
     c_hbm,
     f1_hbm,
     f2_hbm,
-    mixed_hbm,
-    gin_hbm,
-    g1_hbm,
-    g2_hbm,
+    mixed,
+    gin,
+    g1,
+    g2,
     xv,
     cv,
     f1,
@@ -66,14 +66,11 @@
     p2,
     r1,
     r2,
-    g1,
-    g2,
     ssem,
     rsem,
     dssem,
     drsem,
     insem,
-    outsem,
 ):
     sends = (send0, send1, send2, send3)
     recvs = (recv0, recv1, recv2, recv3)
@@ -169,7 +166,7 @@
     def dp_whole(g):
         return dp_copy(g, 0, 0, (ndp - 1) * piece, (dp + 1) % ndp)
 
-    def dp_finish(g, out, out_hbm):
+    def dp_finish(g, out):
         dp_whole(g).wait_recv()
         others[g][pl.ds(own, piece), :] = parts[g][pl.ds(own, piece), :]
         step = min(piece, 128)
@@ -182,9 +179,6 @@
             out[pl.ds(pl.multiple_of(i * step, step), step), :] = total
 
         loop(piece // step, add)
-        copy = pltpu.make_async_copy(out, out_hbm, outsem.at[2 * chunks + g])
-        copy.start()
-        return copy
 
     shift = count.bit_length() - 1
     back_shift = rows.bit_length() - 1
@@ -320,50 +314,49 @@
 
     for n in range(chunks):
         make_product(f1t, recv2, spread, n)
-    outs = [dp_finish(1, g2, g2_hbm)]
+    dp_finish(1, g2)
 
     for n in range(chunks):
         if n == chunks - 1:
-            outs.append(dp_finish(0, g1, g1_hbm))
+            dp_finish(0, g1)
         arrived(SECOND, n)
 
-        def tile(t, n=n):
+        cols = pl.ds(n * width, width)
+
+        def tile(t, n=n, cols=cols):
             s = rowsof(t)
             monarch = recv3[n, s, :].astype(F32)
-            send0[n, s, :] = (xv[n, s, :].astype(F32) * monarch).astype(BF16)
-            send1[n, s, :] = (cv[n, s, :].astype(F32) * monarch + spread[n, s, :]).astype(BF16)
+            mixed[s, cols] = (xv[n, s, :].astype(F32) * monarch).astype(BF16)
+            gin[s, cols] = (cv[n, s, :].astype(F32) * monarch + spread[n, s, :]).astype(BF16)
 
         loop(tiles, tile)
-        cols = pl.ds(n * width, width)
-        for i, (src, dst) in enumerate(((send0, mixed_hbm), (send1, gin_hbm))):
-            copy = pltpu.make_async_copy(src.at[n], dst.at[:, cols], outsem.at[2 * n + i])
-            copy.start()
-            outs.append(copy)
 
     for t, n in units[len(units) - DEPTH :]:
         whole(t, n).wait_send()
     dp_whole(0).wait_send()
     dp_whole(1).wait_send()
-    for copy in outs:
-        copy.wait()
 
 
 def copy_out(*refs):
     half = len(refs) // 2
-    for src, dst in zip(refs[:half], refs[half:]):
-        dst[...] = src[...]
+    sem = refs[-1]
+    copies = [
+        pltpu.make_async_copy(src, dst, sem.at[i])
+        for i, (src, dst) in enumerate(zip(refs[:half], refs[half:-1]))
+    ]
+    for copy in copies:
+        copy.start()
+    for copy in copies:
+        copy.wait()
 
 
 def hand_over(arrays):
-    steps = 4
-    specs = [pl.BlockSpec((a.shape[0] // steps, a.shape[1]), lambda i: (i, 0)) for a in arrays]
     return pl.pallas_call(
         copy_out,
-        grid=(steps,),
-        in_specs=specs,
-        out_specs=specs,
+        in_specs=[pl.BlockSpec(memory_space=pltpu.VMEM)] * len(arrays),
+        out_specs=[pl.BlockSpec(memory_space=pl.ANY)] * len(arrays),
         out_shape=[jax.ShapeDtypeStruct(a.shape, a.dtype) for a in arrays],
-        compiler_params=pltpu.CompilerParams(vmem_limit_bytes=60 * 1024 * 1024),
+        scratch_shapes=[pltpu.SemaphoreType.DMA((len(arrays),))],
     )(*arrays)
 
 
@@ -379,29 +372,27 @@
     results = pl.pallas_call(
         functools.partial(kernel, count, ndp),
         out_shape=(
-            jax.ShapeDtypeStruct((block, width), BF16),
-            jax.ShapeDtypeStruct((block, width), BF16),
-            jax.ShapeDtypeStruct((piece, block), F32),
-            jax.ShapeDtypeStruct((piece, block), F32),
+            pltpu.VMEM((block, width), BF16),
+            pltpu.VMEM((block, width), BF16),
+            pltpu.VMEM((piece, block), F32),
+            pltpu.VMEM((piece, block), F32),
         ),
         in_specs=[spec] * 4,
-        out_specs=[spec] * 4,
+        out_specs=[pl.BlockSpec(memory_space=pltpu.VMEM)] * 4,
         scratch_shapes=[chunked] * 2
         + [square] * 6
         + [chunked] * 8
         + [pltpu.VMEM((CHUNKS, block, cut), F32)]
         + [square] * 4
-        + [pltpu.VMEM((piece, block), F32)] * 2
         + [
             pltpu.SemaphoreType.DMA((4, CHUNKS)),
             pltpu.SemaphoreType.DMA((4, CHUNKS)),
             pltpu.SemaphoreType.DMA((2,)),
             pltpu.SemaphoreType.DMA((2,)),
             pltpu.SemaphoreType.DMA((2 * CHUNKS + 2,)),
-            pltpu.SemaphoreType.DMA((2 * CHUNKS + 2,)),
         ],
         compiler_params=pltpu.CompilerParams(
-            collective_id=0, has_side_effects=True, vmem_limit_bytes=60 * 1024 * 1024
+            collective_id=0, has_side_effects=True, vmem_limit_bytes=54 * 1024 * 1024
         ),
         cost_estimate=pl.CostEstimate(
             flops=12 * block * block * width, bytes_accessed=24 * block * width, transcendentals=0

time: 197 us -> 200 us (1.015)
  local copies, waits for them, and re-layouts: 0 us -> 5.3 us
  Pallas kernels: 196 us -> 194 us
    unnamed x0 -> x8, local copies, waits for them, and re-layouts: none -> 5.3 us
where the time goes in v3:
time: 200 us
  Pallas kernels  194 us (97%)
  local copies, waits for them, and re-layouts  5.3 us (3%)
    pallas_call x1, Pallas kernels, local(): pl.pallas_call(functools.partial(kernel, count, ndp), out_shape=(pltpu.VM...  187 us
    pallas_call x1, Pallas kernels, hand_over(): pl.pallas_call(copy_out, in_specs=[pl.BlockSpec(memory_space=pltpu.VMEM)]...  6.83 us
    unnamed x8, local copies, waits for them, and re-layouts  5.3 us

profile of v3, /device:TPU:16, one launch (start us, length us, event | category | flops | bytes accessed | tf_op | source)
XLA Modules:
  0.0 200.1 jit_solution(8084598232198405240)
XLA Ops:
  0.6 187.3 %shard_map.75 = (bf16[1024,1024]{1,0:T(8,128)(2,1)S(1)}, bf16[1024,1024]{1,0:T(8,128)(2,1)S(1)}, f32[512,1024]{1,0:T(8,128)S(1)}, f32[512,1024]{1,0:T(8,128)S(1)}) custom-call(bf16[1024,1024]{1,0:T(8,128)(2,1)} %bitcast.8, bf16[1024,1024]{1,0:T(8,128)(2,1)} %bitcast.9, bf16[1024,1024]{1,0:T(8,128)(2,1)} %bitcast.10, bf16[1024,1024]{1,0:T(8,128)(2,1)} %bitcast.11), custom_call_target="tpu_custom_call" | custom-call | flops 12884901888 | bytes 25165824 | tf_op jit(solution)/shard_map/pallas_call | solution.py:372
  188.0 0.0 copy-start
  188.0 1.3 copy-done
  189.3 0.0 copy-start.1
  189.3 1.3 copy-done.1
  190.6 0.0 copy-start.2
  190.6 1.3 copy-done.2
  191.9 0.0 copy-start.3
  191.9 1.3 copy-done.3
  193.3 6.8 %shard_map.76 = (bf16[1024,1024]{1,0:T(8,128)(2,1)}, bf16[1024,1024]{1,0:T(8,128)(2,1)}, f32[512,1024]{1,0:T(8,128)}, f32[512,1024]{1,0:T(8,128)}) custom-call(bf16[1024,1024]{1,0:T(8,128)(2,1)} %copy-done, bf16[1024,1024]{1,0:T(8,128)(2,1)} %copy-done.1, f32[512,1024]{1,0:T(8,128)} %copy-done.2, f32[512,1024]{1,0:T(8,128)} %copy-done.3), custom_call_target="tpu_custom_call" | custom-call | tf_op jit(solution)/shard_map/pallas_call | solution.py:354
Async XLA Ops:
  188.0 1.3 copy-start
  189.3 1.3 copy-start.1
  190.6 1.3 copy-start.2
  191.9 1.4 copy-start.3
